TPU v7x, 32 devices: a whole 2x2x4 slice. The times are simulated.
32 devices in a mesh: groups: 2 (over x), graph: 16 (over z, y, core).
Axes of the slice: x: 2, y: 2, z: 4, core: 2. Of those that a mesh axis runs over, the one named last changes fastest.
Arguments:
- var_feat: bfloat16 [65536, 256], P(('groups', 'graph')), parts along dimension 0, may hold values from -6 to 6
- con_feat: bfloat16 [32768, 256], P(('groups', 'graph')), parts along dimension 0, may hold values from -6 to 6
- tile_values: bfloat16 [2048, 128, 128], P(('groups', 'graph')), parts along dimension 0, may hold values from -0.1875 to 0.1875
- tile_row: int32 [2048], P(('groups', 'graph')), parts along dimension 0, may hold values from 0 to 7
- tile_peer: int32 [2048, 1], P(('groups', 'graph')), parts along dimension 0, may hold values from 0 to 15; in each aligned block of 64 rows (0 to 63, 64 to 127, ...) at most 4 rows name the same one
- tile_col: int32 [2048], P(('groups', 'graph')), parts along dimension 0, may hold values from 0 to 15
- labels: int32 [65536], P(('groups', 'graph')), parts along dimension 0, may hold values 0 or 1
- w_msg_var: bfloat16 [256, 256], replicated, may hold values from -0.375 to 0.375
- w_con: bfloat16 [256, 256], replicated, may hold values from -0.375 to 0.375
- w_msg_con: bfloat16 [256, 256], replicated, may hold values from -0.375 to 0.375
- w_var: bfloat16 [256, 256], replicated, may hold values from -0.375 to 0.375
- w_out: bfloat16 [256], replicated, may hold values from -0.375 to 0.375
Outputs:
- logits: float32 [65536], P(('groups', 'graph')), parts along dimension 0
- grad_msg_var: float32 [512, 256], P('groups'), parts along dimension 0
- grad_con: float32 [512, 256], P('groups'), parts along dimension 0
- grad_msg_con: float32 [512, 256], P('groups'), parts along dimension 0
- grad_var: float32 [512, 256], P('groups'), parts along dimension 0
- grad_out: float32 [512], P('groups'), parts along dimension 0
There are 2 independent parts, one for each index of `groups`. A program takes and returns all parts, laid end to end along the dimension named above; an argument that names none is the same for every part. Nothing has to cross between parts.
Inputs may be any that keep to these rules, and one draw needn't show every extreme that they name: Among the 64 tiles held by one device, at most 4 have the same tile_peer; in every draw some device has exactly 4 tiles with one tile_peer.
All inputs are finite; a program needn't handle non-finite values. No bound on the sum of `labels` on one device may be relied on, other than what follows from the above.
Results may differ from a plain program's by a relative error of at most 0.0075.
Values may be sent and summed in bfloat16 or wider, within the bound.
A program may use at most 128 MiB of HBM per device.

v0:
```python
import jax
import jax.numpy as jnp
from jax import lax
from jax.sharding import PartitionSpec as P

TILE_EDGE = 128


def silu_slope(value):
    sig = jax.nn.sigmoid(value)
    return sig * (1.0 + value * (1.0 - sig))


def on_device(
    var_feat,
    con_feat,
    tile_values,
    tile_row,
    tile_peer,
    tile_col,
    labels,
    w_msg_var,
    w_con,
    w_msg_con,
    w_var,
    w_out,
):
    highest = lax.Precision.HIGHEST
    feature_width = var_feat.shape[1]
    blocks_v = var_feat.shape[0] // TILE_EDGE
    blocks_c = con_feat.shape[0] // TILE_EDGE
    count = tile_values.shape[0]
    device_list = lax.axis_size("graph")
    slot_capacity = max(2, count // device_list)
    slot_count = device_list * slot_capacity
    peers = tile_peer[:, 0]
    order = jnp.arange(count, dtype=jnp.int32)
    earlier = (peers[:, None] == peers[None, :]) & (order[None, :] < order[:, None])
    rank = jnp.sum(earlier.astype(jnp.int32), axis=1)
    slot_buffer = peers * slot_capacity + rank
    slot_index = jnp.arange(slot_count, dtype=jnp.int32)
    asked = (
        jnp.sum(
            jnp.where(slot_buffer[:, None] == slot_index[None, :], tile_col[:, None] + 1, 0), axis=0
        )
        - 1
    )
    incoming = lax.all_to_all(
        asked.reshape(device_list, slot_capacity), "graph", split_axis=0, concat_axis=0, tiled=True
    ).reshape(slot_count)
    valid = incoming >= 0
    safe = jnp.where(valid, incoming, 0)
    mask_rows = valid[:, None, None]
    var_blocks = var_feat.reshape(blocks_v, TILE_EDGE, feature_width)

    def to_slots(blocks):
        picked = jnp.take(blocks, safe, axis=0)
        return jnp.where(mask_rows, picked, jnp.zeros((), blocks.dtype)).reshape(
            device_list, slot_capacity, TILE_EDGE, feature_width
        )

    received_tiles = lax.all_to_all(
        to_slots(var_blocks), "graph", split_axis=0, concat_axis=0, tiled=True
    )
    tile_input = jnp.take(
        received_tiles.reshape(slot_count, TILE_EDGE, feature_width), slot_buffer, axis=0
    )
    tile_u = jnp.einsum(
        "tbi,ij->tbj", tile_input, w_msg_var, preferred_element_type=jnp.float32
    ).astype(jnp.bfloat16)
    messages = jnp.einsum("tij,tjd->tid", tile_values, tile_u, preferred_element_type=jnp.float32)
    row_hot = (tile_row[None, :] == jnp.arange(blocks_c, dtype=jnp.int32)[:, None]).astype(
        jnp.float32
    )
    summed = jnp.einsum("ct,tbd->cbd", row_hot, messages, precision=highest)
    con_pre = summed.reshape(blocks_c * TILE_EDGE, feature_width) + jnp.dot(
        con_feat, w_con, preferred_element_type=jnp.float32
    )
    con_act = jax.nn.silu(con_pre).astype(jnp.bfloat16)
    proj_con = jnp.dot(con_act, w_msg_con, preferred_element_type=jnp.float32).astype(jnp.bfloat16)
    tile_q = jnp.take(proj_con.reshape(blocks_c, TILE_EDGE, feature_width), tile_row, axis=0)
    return_trip = jnp.einsum(
        "tji,tjd->tid", tile_values, tile_q, preferred_element_type=jnp.float32
    ).astype(jnp.bfloat16)
    outgoing_tiles = (
        jnp.zeros((slot_count, TILE_EDGE, feature_width), jnp.bfloat16)
        .at[slot_buffer]
        .set(return_trip)
    )
    returned_tiles = lax.all_to_all(
        outgoing_tiles.reshape(device_list, slot_capacity, TILE_EDGE, feature_width),
        "graph",
        split_axis=0,
        concat_axis=0,
        tiled=True,
    )
    block_hot = (
        (safe[None, :] == jnp.arange(blocks_v, dtype=jnp.int32)[:, None]) & valid[None, :]
    ).astype(jnp.bfloat16)
    gathered = jnp.einsum(
        "vs,sbd->vbd",
        block_hot,
        returned_tiles.reshape(slot_count, TILE_EDGE, feature_width),
        preferred_element_type=jnp.float32,
    )
    var_pre = gathered.reshape(blocks_v * TILE_EDGE, feature_width) + jnp.dot(
        var_feat, w_var, preferred_element_type=jnp.float32
    )
    var_act = jax.nn.silu(var_pre)
    out_vec = w_out.astype(jnp.float32)
    logits = jnp.dot(var_act, out_vec, precision=highest)
    scale = 1.0 / jnp.sqrt(jnp.float32(device_list * var_feat.shape[0]))
    dlog = (jax.nn.sigmoid(logits) - labels.astype(jnp.float32)) * scale
    grad_out_part = jnp.dot(dlog, var_act, precision=highest)
    dvar = (dlog[:, None] * out_vec[None, :] * silu_slope(var_pre)).astype(jnp.bfloat16)
    grad_var_part = jnp.einsum("ri,rj->ij", var_feat, dvar, preferred_element_type=jnp.float32)
    received_gradients = lax.all_to_all(
        to_slots(dvar.reshape(blocks_v, TILE_EDGE, feature_width)),
        "graph",
        split_axis=0,
        concat_axis=0,
        tiled=True,
    )
    tile_weight_gradient = jnp.take(
        received_gradients.reshape(slot_count, TILE_EDGE, feature_width), slot_buffer, axis=0
    )
    dmsg = jnp.einsum(
        "tij,tjd->tid", tile_values, tile_weight_gradient, preferred_element_type=jnp.float32
    )
    dproj_con = (
        jnp.einsum("ct,tbd->cbd", row_hot, dmsg, precision=highest)
        .reshape(blocks_c * TILE_EDGE, feature_width)
        .astype(jnp.bfloat16)
    )
    grad_msg_con_part = jnp.einsum(
        "ri,rj->ij", con_act, dproj_con, preferred_element_type=jnp.float32
    )
    dcon_pre = jnp.einsum("rj,ij->ri", dproj_con, w_msg_con, preferred_element_type=jnp.float32)
    dcon = (dcon_pre * silu_slope(con_pre)).astype(jnp.bfloat16)
    grad_con_part = jnp.einsum("ri,rj->ij", con_feat, dcon, preferred_element_type=jnp.float32)
    tile_dm = jnp.take(dcon.reshape(blocks_c, TILE_EDGE, feature_width), tile_row, axis=0)
    tile_du = jnp.einsum(
        "tij,tid->tjd", tile_values, tile_dm, preferred_element_type=jnp.float32
    ).astype(jnp.bfloat16)
    grad_msg_var_part = jnp.einsum(
        "tbi,tbj->ij", tile_input, tile_du, preferred_element_type=jnp.float32
    )
    totals = lax.psum(
        (grad_msg_var_part, grad_con_part, grad_msg_con_part, grad_var_part, grad_out_part), "graph"
    )
    return (logits, totals[0], totals[1], totals[2], totals[3], totals[4])


def solution(mesh):
    return jax.shard_map(
        on_device,
        mesh=mesh,
        in_specs=(
            P(("groups", "graph"), None),
            P(("groups", "graph"), None),
            P(("groups", "graph"), None, None),
            P(("groups", "graph")),
            P(("groups", "graph"), None),
            P(("groups", "graph")),
            P(("groups", "graph")),
            P(),
            P(),
            P(),
            P(),
            P(),
        ),
        out_specs=(
            P(("groups", "graph")),
            P("groups", None),
            P("groups", None),
            P("groups", None),
            P("groups", None),
            P("groups"),
        ),
        check_vma=False,
    )
```

profile of v0, /device:TPU:0, one launch (start us, length us, event | category | flops | bytes accessed | tf_op | source)
XLA Modules:
  0.0 566.4 jit_solution(14014676683705723656)
XLA Ops:
  9.7 13.6 %all_to_all.21 = s32[16,1,4]{2,1,0:T(1,128)S(1)} all-to-all(s32[16,1,4]{2,1,0:T(1,128)S(1)} %bitcast.95), channel_id=1, replica_groups=mesh['groups'=2,'graph'=16] {'graph'}, dimensions={0} | all-to-all | bytes 512 | tf_op jit(solution)/shard_map/all_to_all | solution.py:48
  32.6 4.7 all-to-all-start.1
  37.3 77.5 %all-to-all-done.1 = bf16[16,4,128,256]{3,2,1,0:T(8,128)(2,1)} async-done(((bf16[16,4,128,256]{3,2,1,0:T(8,128)(2,1)}), bf16[16,4,128,256]{3,2,1,0:T(8,128)(2,1)}, u32[]{:S(2)}, u32[]{:S(2)}) %all-to-all-start.1) | async-done | bytes 4194336 | tf_op jit(solution)/shard_map/all_to_all | solution.py:62
  114.9 5.0 gather_fusion.1
  119.9 8.0 %fusion.14 = f32[64,128,256]{1,2,0:T(8,128)} fusion(bf16[64,128,128]{2,1,0:T(8,128)(2,1)S(1)} %copy-done, bf16[64,128,256]{2,1,0:T(8,128)(2,1)} %gather_fusion.1, pred[64]{0:T(512)(128)(4,1)S(1)} %get-tuple-element.43, bf16[256,256]{1,0:T(8,128)(2,1)S(1)} %copy-done.7), kind=kOutput, calls=%fused_computation.25 | convolution fusion | flops 1614807040 | bytes 14811200 | tf_op jit(solution)/shard_map/tij,tjd->tid/dot_general | solution.py:71
  127.9 9.2 %copy.65 = f32[64,128,256]{2,0,1:T(8,128)} copy(f32[64,128,256]{1,2,0:T(8,128)} %fusion.14) | data formatting | bytes 16777216 | tf_op jit(solution)/shard_map/tij,tjd->tid/dot_general | solution.py:71
  137.1 5.2 fusion.53
  147.9 5.6 convert_bitcast_fusion
  153.5 6.4 %copy.68 = bf16[64,128,256]{2,1,0:T(8,128)(2,1)} copy(bf16[64,128,256]{1,2,0:T(8,128)(2,1)} %convert_bitcast_fusion) | data formatting | bytes 8388608 | tf_op jit(solution)/shard_map/convert_element_type | solution.py:84
  162.3 12.0 %scatter_fusion = bf16[64,128,256]{2,1,0:T(8,128)(2,1)} fusion(bf16[64,128,256]{2,1,0:T(8,128)(2,1)} %broadcast_in_dim.74, s32[64]{0:T(128)S(1)} %get-tuple-element.48, bf16[64,128,256]{2,1,0:T(8,128)(2,1)} %copy.68), kind=kCustom, calls=%fused_computation.6 | custom fusion | bytes 12583168 | tf_op jit(solution)/shard_map/scatter | solution.py:88
  174.3 7.7 %copy.69 = bf16[16,4,128,256]{3,1,2,0:T(4,128)(2,1)} copy(bf16[16,4,128,256]{3,2,1,0:T(8,128)(2,1)} %bitcast.85) | data formatting | bytes 8388608 | tf_op jit(solution)/shard_map/reshape | solution.py:91
  182.0 19.8 %all-to-all-start.2 = ((bf16[16,4,128,256]{3,1,2,0:T(4,128)(2,1)}), bf16[16,4,128,256]{3,1,2,0:T(4,128)(2,1)}, u32[]{:S(2)}, u32[]{:S(2)}) async-start(bf16[16,4,128,256]{3,1,2,0:T(4,128)(2,1)} %copy.69), calls=%async_computation.2 | async-start | bytes 8388608 | tf_op jit(solution)/shard_map/all_to_all | solution.py:90
  201.8 77.6 %all-to-all-done.2 = bf16[16,4,128,256]{3,1,2,0:T(4,128)(2,1)} async-done(((bf16[16,4,128,256]{3,1,2,0:T(4,128)(2,1)}), bf16[16,4,128,256]{3,1,2,0:T(4,128)(2,1)}, u32[]{:S(2)}, u32[]{:S(2)}) %all-to-all-start.2) | async-done | bytes 4194336 | tf_op jit(solution)/shard_map/all_to_all | solution.py:90
  279.5 6.5 %copy.70 = bf16[16,4,128,256]{3,1,0,2:T(4,128)(2,1)} copy(bf16[16,4,128,256]{3,1,2,0:T(4,128)(2,1)} %all-to-all-done.2) | data formatting | bytes 8388608 | tf_op jit(solution)/shard_map/all_to_all | solution.py:90
  286.0 6.9 %reshape.120 = bf16[64,128,256]{2,0,1:T(8,128)(2,1)} reshape(bf16[16,4,128,256]{3,1,0,2:T(4,128)(2,1)} %copy.70) | data formatting | bytes 8388608 | tf_op jit(solution)/shard_map/reshape | solution.py:103
  306.6 19.7 %all-to-all-start.3 = ((bf16[16,4,128,256]{3,2,1,0:T(8,128)(2,1)}), bf16[16,4,128,256]{3,2,1,0:T(8,128)(2,1)}, u32[]{:S(2)}, u32[]{:S(2)}) async-start(bf16[16,4,128,256]{3,2,1,0:T(8,128)(2,1)} %bitcast.89), calls=%async_computation.3 | async-start | bytes 8388608 | tf_op jit(solution)/shard_map/all_to_all | solution.py:117
  329.0 75.0 %all-to-all-done.3 = bf16[16,4,128,256]{3,2,1,0:T(8,128)(2,1)} async-done(((bf16[16,4,128,256]{3,2,1,0:T(8,128)(2,1)}), bf16[16,4,128,256]{3,2,1,0:T(8,128)(2,1)}, u32[]{:S(2)}, u32[]{:S(2)}) %all-to-all-start.3) | async-done | bytes 4194336 | tf_op jit(solution)/shard_map/all_to_all | solution.py:117
  404.0 5.0 gather_fusion.4
  409.0 6.8 %fusion.19 = f32[64,128,256]{1,2,0:T(8,128)} fusion(bf16[64,128,128]{2,1,0:T(8,128)(2,1)S(1)} %copy-done, bf16[64,128,256]{2,1,0:T(8,128)(2,1)} %gather_fusion.4, pred[64]{0:T(512)(128)(4,1)S(1)} %get-tuple-element.43), kind=kOutput, calls=%fused_computation.27 | convolution fusion | flops 538968064 | bytes 14680128 | tf_op jit(solution)/shard_map/tij,tjd->tid/dot_general | solution.py:127
  415.8 9.2 %copy.73 = f32[64,128,256]{2,0,1:T(8,128)} copy(f32[64,128,256]{1,2,0:T(8,128)} %fusion.19) | data formatting | bytes 16777216 | tf_op jit(solution)/shard_map/tij,tjd->tid/dot_general | solution.py:127
  425.0 6.3 %convolution_convert_fusion.1 = bf16[8,128,256]{2,0,1:T(8,128)(2,1)S(1)} fusion(f32[64,128,256]{2,0,1:T(8,128)} %copy.73, s32[64]{0:T(128)S(1)} %copy-done.12), kind=kOutput, calls=%fused_computation.39 | convolution fusion | flops 201589248 | bytes 8913152 | tf_op jit(solution)/shard_map/ct,tbd->cbd/dot_general | solution.py:131
  436.8 7.0 %fusion.34 = f32[256,256]{1,0:T(8,128)} fusion(bf16[64,128,128]{2,1,0:T(8,128)(2,1)S(1)} %copy-done, bf16[64,128,256]{2,1,0:T(8,128)(2,1)} %gather_fusion.5, pred[64]{0:T(512)(128)(4,1)S(1)} %get-tuple-element.52, bf16[64,128,256]{2,1,0:T(8,128)(2,1)} %gather_fusion.1, pred[64]{0:T(512)(128)(4,1)S(1)} %get-tuple-element.43), kind=kOutput, calls=%fused_computation.41 | convolution fusion | flops 1616904192 | bytes 10748032 | tf_op jit(solution)/shard_map/tbi,tbj->ij/dot_general | solution.py:145
  446.7 48.6 %psum.39 = f32[256]{0:T(256)} all-reduce(f32[256]{0:T(256)S(1)} %bitcast.99), channel_id=1, replica_groups=mesh['groups'=2,'graph'=16] {'graph'}, use_global_device_ids=true, to_apply=%region_7.11 | all-reduce | flops 256 | bytes 2048 | tf_op jit(solution)/shard_map/psum | solution.py:148
  495.3 57.3 %all-reduce.3.cloned.1.call-done = (f32[256,256]{1,0:T(8,128)}, f32[256,256]{0,1:T(8,128)}, f32[256,256]{1,0:T(8,128)}, f32[256,256]{0,1:T(8,128)}) async-done(((f32[256,256]{1,0:T(8,128)}, f32[256,256]{0,1:T(8,128)}, f32[256,256]{1,0:T(8,128)}, f32[256,256]{0,1:T(8,128)}), (f32[256,256]{1,0:T(8,128)}, f32[256,256]{0,1:T(8,128)}, f32[256,256]{1,0:T(8,128)}, ...) | async-done | bytes 1048592 | tf_op jit(solution)/shard_map/psum | solution.py:148
  (80 shorter events, 51.5 us)
Async XLA Ops:
  7.2 112.7 %copy-start = (bf16[64,128,128]{2,1,0:T(8,128)(2,1)S(1)}, bf16[64,128,128]{2,1,0:T(8,128)(2,1)}, u32[]{:S(2)}) copy-start(bf16[64,128,128]{2,1,0:T(8,128)(2,1)} %param.20) | copy-start | bytes 6291460
  32.6 4.7 copy-start.12
  32.6 4.7 copy-start.13
  32.6 82.3 %all-to-all-start.1 = ((bf16[16,4,128,256]{3,2,1,0:T(8,128)(2,1)}), bf16[16,4,128,256]{3,2,1,0:T(8,128)(2,1)}, u32[]{:S(2)}, u32[]{:S(2)}) async-start(bf16[16,4,128,256]{3,2,1,0:T(8,128)(2,1)} %bitcast.88), calls=%async_computation.1 | async-start | bytes 8388608 | tf_op jit(solution)/shard_map/all_to_all | solution.py:62
  114.9 5.0 copy-start.7
  137.1 5.6 copy-start.5
  137.1 5.6 copy-start.14
  142.3 2.5 copy-start.8
  144.0 0.8 copy-start.3
  182.0 19.8 %copy-start.15 = (bf16[256]{0:T(256)(128)(2,1)S(1)}, bf16[256]{0:T(256)(128)(2,1)}, u32[]{:S(2)}) copy-start(bf16[256]{0:T(256)(128)(2,1)} %param.29) | copy-start | bytes 1540
  182.0 97.5 %all-to-all-start.2 = ((bf16[16,4,128,256]{3,1,2,0:T(4,128)(2,1)}), bf16[16,4,128,256]{3,1,2,0:T(4,128)(2,1)}, u32[]{:S(2)}, u32[]{:S(2)}) async-start(bf16[16,4,128,256]{3,1,2,0:T(4,128)(2,1)} %copy.69), calls=%async_computation.2 | async-start | bytes 8388608 | tf_op jit(solution)/shard_map/all_to_all | solution.py:90
  292.9 4.2 copy-start.1
  292.9 4.2 copy-start.9
  297.5 1.5 copy-start.2
  297.6 1.5 copy-start.10
  299.0 3.6 copy-start.11
  306.6 97.4 %all-to-all-start.3 = ((bf16[16,4,128,256]{3,2,1,0:T(8,128)(2,1)}), bf16[16,4,128,256]{3,2,1,0:T(8,128)(2,1)}, u32[]{:S(2)}, u32[]{:S(2)}) async-start(bf16[16,4,128,256]{3,2,1,0:T(8,128)(2,1)} %bitcast.89), calls=%async_computation.3 | async-start | bytes 8388608 | tf_op jit(solution)/shard_map/all_to_all | solution.py:117
  326.3 226.3 %all-reduce.3.cloned.1.call-start = ((), (), s32[]{:S(2)}) async-start(), calls=%async_computation.4 | async-start | bytes 2097152 | tf_op jit(solution)/shard_map/psum | solution.py:148
  425.0 6.4 %copy-start.4 = (bf16[1024,256]{1,0:T(8,128)(2,1)S(1)}, bf16[1024,256]{1,0:T(8,128)(2,1)}, u32[]{:S(2)}) copy-start(bf16[1024,256]{1,0:T(8,128)(2,1)} %copy-done.3) | copy-start | bytes 1572868
  425.0 7.5 %copy-start.16 = (f32[1024,256]{1,0:T(8,128)S(1)}, f32[1024,256]{1,0:T(8,128)}, u32[]{:S(2)}) copy-start(f32[1024,256]{1,0:T(8,128)} %get-tuple-element.51) | copy-start | bytes 3145732
  431.2 1.7 copy-start.6
Sparse Core Ops, SparseCore 0:
  443.9 108.6 all-reduce.2
where the time goes:
time: 568 us; the launch traced here: 566 us
  waiting for transfers between devices  287 us (51%)
  local copies, waits for them, and re-layouts  92.7 us (16%)
  blocking collectives  62.2 us (11%)
  matrix products  53.3 us (9%)
  starting transfers between devices  44.4 us (8%)
  between operations  14.3 us (3%)
  other arithmetic  11.9 us (2%)
    all_to_all x1, waiting for transfers between devices, on_device(): lax.all_to_all(outgoing_tiles.reshape(device_list, slot_capacity, TILE_ED...  77.6 us
    all_to_all x1, waiting for transfers between devices, on_device(): lax.all_to_all(to_slots(var_blocks), 'graph', split_axis=0, concat_axis=0...  77.5 us
    all_to_all x1, waiting for transfers between devices, on_device(): lax.all_to_all(to_slots(dvar.reshape(blocks_v, TILE_EDGE, feature_width))...  75 us
    psum x1, waiting for transfers between devices, on_device(): lax.psum((grad_msg_var_part, grad_con_part, grad_msg_con_part, grad_var_p...  57.3 us
    psum x1, blocking collectives, on_device(): lax.psum((grad_msg_var_part, grad_con_part, grad_msg_con_part, grad_var_p...  48.6 us
    all_to_all x1, starting transfers between devices, on_device(): lax.all_to_all(outgoing_tiles.reshape(device_list, slot_capacity, TILE_ED...  19.8 us
    all_to_all x1, starting transfers between devices, on_device(): lax.all_to_all(to_slots(dvar.reshape(blocks_v, TILE_EDGE, feature_width))...  19.7 us
    all_to_all x1, blocking collectives, on_device(): lax.all_to_all(asked.reshape(device_list, slot_capacity), 'graph', split_...  13.6 us
  transfers between devices with their start and end apart: 4, of which 4 were waited for; matrix products, arithmetic and copies ran while one was open for 1% of the time, Pallas kernels for 0%

commit v1 on v0

v1 whole, which is shorter than its diff:
```python
import functools

import jax
import jax.numpy as jnp
from jax import lax
from jax.experimental import pallas as pl
from jax.experimental.pallas import tpu as pltpu
from jax.sharding import PartitionSpec as P

EDGE = 128
GROUP = 4
F32 = jnp.float32
BF16 = jnp.bfloat16


def dot(a, b):
    return jnp.dot(a, b, preferred_element_type=F32)


def silu_slope(value):
    sig = jax.nn.sigmoid(value)
    return sig * (1.0 + value * (1.0 - sig))


def kernel(
    n,
    cap,
    slot_tile,
    slot_row,
    asked_of_me,
    var_feat,
    con_feat,
    tiles,
    labels,
    w_msg_var,
    w_con,
    w_msg_con,
    w_var,
    w_out,
    logits_out,
    grads_out,
    grad_out_out,
    send,
    got_feat,
    got_back,
    got_dvar,
    slot_mat,
    slot_mat_t,
    feat_t,
    con_feat_t,
    con_act_t,
    var_acc,
    con_acc,
    con_slope,
    con_half,
    dvar,
    grads,
    part_got,
    part_sum,
    total_got,
    head_part,
    head_got,
    send_sem,
    feat_sem,
    back_sem,
    dvar_sem,
    part_sem,
    total_sem,
    head_send_sem,
    head_sem,
):
    me = lax.axis_index("graph")
    lane = lax.axis_index("groups")
    blocks_v = var_feat.shape[0]
    blocks_c = con_feat.shape[0]
    scale = 1.0 / jnp.sqrt(jnp.float32(n * blocks_v * EDGE))
    turned = feat_t.shape[0] == n

    def each_peer(body):
        def step(i, carry):
            body(lax.rem(me + i, n))
            return carry

        lax.fori_loop(1, n, step, 0)

    def each_sender(body):
        def step(i, carry):
            body(lax.rem(me + n - i, n))
            return carry

        lax.fori_loop(1, n, step, 0)

    def loop(count, body):
        def step(i, carry):
            body(i)
            return carry

        lax.fori_loop(0, count, step, 0)

    def copy_to(peer, source, target, out_sem, in_sem):
        return pltpu.make_async_remote_copy(
            src_ref=source,
            dst_ref=target.at[me],
            send_sem=out_sem.at[peer],
            recv_sem=in_sem.at[me],
            device_id=(lane, peer),
            device_id_type=pl.DeviceIdType.MESH,
        )

    def copy_from(peer, source, target, out_sem, in_sem):
        return pltpu.make_async_remote_copy(
            src_ref=source,
            dst_ref=target.at[peer],
            send_sem=out_sem.at[peer],
            recv_sem=in_sem.at[peer],
            device_id=(lane, peer),
            device_id_type=pl.DeviceIdType.MESH,
        )

    barrier = pltpu.get_barrier_semaphore()

    def greet(peer):
        pl.semaphore_signal(
            barrier, inc=1, device_id=(lane, peer), device_id_type=pl.DeviceIdType.MESH
        )

    each_peer(greet)
    pl.semaphore_wait(barrier, n - 1)

    def span(c):
        return slice(c * EDGE, (c + 1) * EDGE)

    def fill(source, target, peer):
        for c in range(cap):
            index = jnp.maximum(asked_of_me[peer * cap + c], 0)
            target[peer, span(c), :] = source[index]

    def send_feat(peer):
        fill(var_feat, send, peer)
        copy_to(peer, send.at[peer], got_feat, send_sem, feat_sem).start()

    each_peer(send_feat)
    fill(var_feat, got_feat, me)

    def order_tiles(p):
        for c in range(cap):
            slot = p * cap + c
            index = slot_tile[slot]
            keep = jnp.where(index >= 0, 1.0, 0.0)
            mat = tiles[jnp.maximum(index, 0)].astype(F32) * keep
            slot_mat[slot] = mat.astype(BF16)
            slot_mat_t[slot] = mat.T.astype(BF16)

    loop(n, order_tiles)

    def self_var(b):
        var_acc[b] = dot(var_feat[b], w_var[...])

    loop(blocks_v, self_var)

    def self_con(b):
        con_acc[b] = dot(con_feat[b], w_con[...])
        con_feat_t[b] = con_feat[b].astype(F32).T.astype(BF16)

    loop(blocks_c, self_con)

    def placed(first, peer, block_of, place_of):
        rows = []
        for k in range(GROUP):
            row = []
            for c in range(cap):
                slot = peer * cap + c
                keep = jnp.where(place_of[slot] == first + k, 1.0, 0.0)
                row.append((block_of(slot) * keep).astype(BF16))
            rows.append(jnp.concatenate(row, axis=1))
        return jnp.concatenate(rows, axis=0)

    def tile_block(slot):
        return slot_mat[slot].astype(F32)

    def add_rows(acc, peer, values):
        for g in range(blocks_c // GROUP):
            part = dot(placed(g * GROUP, peer, tile_block, slot_row), values)
            acc[g * GROUP : (g + 1) * GROUP] += part.reshape(GROUP, EDGE, part.shape[1])

    def use_feat(peer):
        proj = dot(got_feat[peer], w_msg_var[...]).astype(BF16)
        add_rows(con_acc, peer, proj)

    use_feat(me)

    def take_feat(peer):
        copy_from(peer, send.at[peer], got_feat, send_sem, feat_sem).wait_recv()
        use_feat(peer)

    each_sender(take_feat)

    def activate(b):
        act = jax.nn.silu(con_acc[b])
        con_act_t[b] = act.T.astype(BF16)
        con_half[b] = dot(act.astype(BF16), w_msg_con[...]).astype(BF16)

    loop(blocks_c, activate)

    each_peer(lambda p: copy_to(p, send.at[p], got_feat, send_sem, feat_sem).wait_send())

    def back_to(peer, target):
        for c in range(cap):
            slot = peer * cap + c
            value = dot(slot_mat_t[slot], con_half[slot_row[slot]])
            target[peer, span(c), :] = value.astype(BF16)

    def send_back(peer):
        back_to(peer, send)
        copy_to(peer, send.at[peer], got_back, send_sem, back_sem).start()

    each_peer(send_back)
    back_to(me, got_back)

    def turn_feat(p):
        feat_t[p] = got_feat[p].astype(F32).T.astype(BF16)

    if turned:
        loop(n, turn_feat)

    def slope_of(b):
        con_slope[b] = silu_slope(con_acc[b])
        con_acc[b] = jnp.zeros_like(con_acc[b])

    loop(blocks_c, slope_of)

    eye = (
        lax.broadcasted_iota(jnp.int32, (EDGE, EDGE), 0)
        == lax.broadcasted_iota(jnp.int32, (EDGE, EDGE), 1)
    ).astype(F32)

    def use_back(peer):
        values = got_back[peer]

        def some(g):
            part = dot(placed(g * GROUP, peer, lambda slot: eye, asked_of_me), values)
            here = pl.ds(g * GROUP, GROUP)
            var_acc[here] = var_acc[here] + part.reshape(GROUP, EDGE, part.shape[1])

        loop(blocks_v // GROUP, some)

    use_back(me)

    def take_back(peer):
        copy_from(peer, send.at[peer], got_back, send_sem, back_sem).wait_recv()
        use_back(peer)

    each_sender(take_back)

    head = w_out[...]
    head_part[...] = jnp.zeros_like(head_part)

    def finish_var(b):
        pre = var_acc[b]
        sig = jax.nn.sigmoid(pre)
        act = pre * sig
        logit = jnp.sum(act * head, axis=1, keepdims=True)
        logits_out[b] = logit
        dlog = (jax.nn.sigmoid(logit) - labels[b].astype(F32)) * scale
        head_part[0:1, :] = head_part[0:1, :] + jnp.sum(dlog * act, axis=0, keepdims=True)
        slope = sig * (1.0 + pre * (1.0 - sig))
        dvar[b] = (dlog * head * slope).astype(BF16)

    loop(blocks_v, finish_var)

    each_peer(lambda p: copy_to(p, send.at[p], got_back, send_sem, back_sem).wait_send())

    def send_dvar(peer):
        fill(dvar, send, peer)
        copy_to(peer, send.at[peer], got_dvar, send_sem, dvar_sem).start()
        copy_to(peer, head_part, head_got, head_send_sem, head_sem).start()

    each_peer(send_dvar)
    fill(dvar, got_dvar, me)
    head_got[me] = head_part[...]

    chunk = grads.shape[1]
    width = w_con.shape[0]
    per = width // chunk

    def keep_grad(which, value):
        grads[which * per : (which + 1) * per] = value.astype(BF16).reshape(
            per, chunk, value.shape[1]
        )

    def grad_var_step(b, total):
        return total + dot(var_feat[b].astype(F32).T.astype(BF16), dvar[b])

    zero = jnp.zeros((width, w_con.shape[1]), F32)
    keep_grad(3, lax.fori_loop(0, blocks_v, grad_var_step, zero))

    add_rows(con_acc, me, got_dvar[me])

    def take_dvar(peer):
        copy_from(peer, send.at[peer], got_dvar, send_sem, dvar_sem).wait_recv()
        add_rows(con_acc, peer, got_dvar[peer])

    each_sender(take_dvar)

    grad_a = zero
    grad_b = zero
    for b in range(blocks_c):
        dproj = con_acc[b].astype(BF16)
        grad_a = grad_a + dot(con_act_t[b], dproj)
        dcon_pre = lax.dot_general(
            dproj, w_msg_con[...], (((1,), (1,)), ((), ())), preferred_element_type=F32
        )
        dcon = (dcon_pre * con_slope[b]).astype(BF16)
        con_half[b] = dcon
        grad_b = grad_b + dot(con_feat_t[b], dcon)
    keep_grad(2, grad_a)
    keep_grad(1, grad_b)

    def grad_msg_step(p, total):
        parts = []
        for c in range(cap):
            slot = p * cap + c
            parts.append(dot(slot_mat_t[slot], con_half[slot_row[slot]]).astype(BF16))
        if turned:
            left = feat_t[p]
        else:
            left = got_feat[p].astype(F32).T.astype(BF16)
        return total + dot(left, jnp.concatenate(parts, axis=0))

    keep_grad(0, lax.fori_loop(0, n, grad_msg_step, zero))

    each_peer(lambda p: copy_to(p, send.at[p], got_dvar, send_sem, dvar_sem).wait_send())
    each_peer(
        lambda p: copy_to(p, grads.at[p], part_got, send_sem, part_sem).start()
    )
    part_got[me] = grads[me]

    each_sender(
        lambda p: copy_from(p, head_part, head_got, head_send_sem, head_sem).wait()
    )
    grad_out_out[...] = jnp.sum(head_got[...], axis=0)

    each_sender(
        lambda p: copy_from(p, grads.at[p], part_got, send_sem, part_sem).wait()
    )

    def add_part(p, total):
        return total + part_got[p].astype(F32)

    total = lax.fori_loop(0, n, add_part, jnp.zeros(part_sum.shape, F32))
    part_sum[...] = total.astype(BF16)
    each_peer(lambda p: copy_to(p, part_sum, total_got, send_sem, total_sem).start())
    total_got[me] = part_sum[...]
    each_sender(
        lambda p: copy_from(p, part_sum, total_got, send_sem, total_sem).wait()
    )
    grads_out[...] = total_got[...]


def on_device(
    var_feat,
    con_feat,
    tile_values,
    tile_row,
    tile_peer,
    tile_col,
    labels,
    w_msg_var,
    w_con,
    w_msg_con,
    w_var,
    w_out,
):
    width = var_feat.shape[1]
    blocks_v = var_feat.shape[0] // EDGE
    blocks_c = con_feat.shape[0] // EDGE
    count = tile_values.shape[0]
    n = lax.axis_size("graph")
    cap = max(2, count // n)
    slots = n * cap
    peers = tile_peer[:, 0]
    order = jnp.arange(count, dtype=jnp.int32)
    earlier = (peers[:, None] == peers[None, :]) & (order[None, :] < order[:, None])
    rank = jnp.sum(earlier.astype(jnp.int32), axis=1)
    place = peers * cap + rank
    hit = place[:, None] == jnp.arange(slots, dtype=jnp.int32)[None, :]

    def by_slot(values):
        return jnp.sum(jnp.where(hit, values[:, None], 0), axis=0)

    asked = by_slot(tile_col + 1) - 1
    slot_tile = by_slot(order + 1) - 1
    slot_row = by_slot(tile_row)
    incoming = lax.all_to_all(
        asked.reshape(n, cap), "graph", split_axis=0, concat_axis=0, tiled=True
    ).reshape(slots)

    wide = cap * EDGE
    chunk = 4 * width // n
    vmem = pl.BlockSpec(memory_space=pltpu.VMEM)
    smem = pl.BlockSpec(memory_space=pltpu.SMEM)
    dma = pltpu.SemaphoreType.DMA((n,))
    logits, grads, grad_out = pl.pallas_call(
        functools.partial(kernel, n, cap),
        out_shape=(
            jax.ShapeDtypeStruct((blocks_v, EDGE, 1), F32),
            jax.ShapeDtypeStruct((n, chunk, width), BF16),
            jax.ShapeDtypeStruct((8, width), F32),
        ),
        in_specs=[smem] * 3 + [vmem] * 9,
        out_specs=(vmem, vmem, vmem),
        scratch_shapes=[
            pltpu.VMEM((n, wide, width), BF16),
            pltpu.VMEM((n, wide, width), BF16),
            pltpu.VMEM((n, wide, width), BF16),
            pltpu.VMEM((n, wide, width), BF16),
            pltpu.VMEM((slots, EDGE, EDGE), BF16),
            pltpu.VMEM((slots, EDGE, EDGE), BF16),
            pltpu.VMEM((n if slots <= count else 1, width, wide), BF16),
            pltpu.VMEM((blocks_c, width, EDGE), BF16),
            pltpu.VMEM((blocks_c, width, EDGE), BF16),
            pltpu.VMEM((blocks_v, EDGE, width), F32),
            pltpu.VMEM((blocks_c, EDGE, width), F32),
            pltpu.VMEM((blocks_c, EDGE, width), F32),
            pltpu.VMEM((blocks_c, EDGE, width), BF16),
            pltpu.VMEM((blocks_v, EDGE, width), BF16),
            pltpu.VMEM((n, chunk, width), BF16),
            pltpu.VMEM((n, chunk, width), BF16),
            pltpu.VMEM((chunk, width), BF16),
            pltpu.VMEM((n, chunk, width), BF16),
            pltpu.VMEM((8, width), F32),
            pltpu.VMEM((n, 8, width), F32),
            dma,
            dma,
            dma,
            dma,
            dma,
            dma,
            dma,
            dma,
        ],
        compiler_params=pltpu.CompilerParams(
            collective_id=0, has_side_effects=True, vmem_limit_bytes=60 * 2**20
        ),
    )(
        slot_tile,
        slot_row,
        incoming,
        var_feat.reshape(blocks_v, EDGE, width),
        con_feat.reshape(blocks_c, EDGE, width),
        tile_values,
        labels.reshape(blocks_v, EDGE, 1),
        w_msg_var,
        w_con,
        w_msg_con,
        w_var,
        w_out.astype(F32).reshape(1, width),
    )
    grads = grads.astype(F32).reshape(4, width, width)
    return (
        logits.reshape(blocks_v * EDGE),
        grads[0],
        grads[1],
        grads[2],
        grads[3],
        grad_out[0],
    )


def solution(mesh):
    rows = P(("groups", "graph"))
    whole = P("groups")
    return jax.shard_map(
        on_device,
        mesh=mesh,
        in_specs=(rows,) * 7 + (P(),) * 5,
        out_specs=(rows,) + (whole,) * 5,
        check_vma=False,
    )
```

time: 568 us -> 357 us (0.63)
  Pallas kernels: 0 us -> 330 us
  waiting for transfers between devices: 287 us -> 2.54 us
  local copies, waits for them, and re-layouts: 92.7 us -> 7.28 us
  blocking collectives: 62.2 us -> 0 us
  matrix products: 53.3 us -> 0 us
  starting transfers between devices: 44.4 us -> 7.39 us
  between operations: 14.3 us -> 0.67 us
    pallas_call x0 -> x1, Pallas kernels: none -> 330 us  [on_device(): pl.pallas_call(functools.partial(kernel, n, cap), out_shape=(jax.ShapeDty...]
    all_to_all x3 -> x1, waiting for transfers between devices: 230 us -> 2.54 us  [on_device(): lax.all_to_all(asked.reshape(n, cap), 'graph', split_axis=0, concat_axis=...]
    psum x1 -> x0, waiting for transfers between devices: 57.3 us -> none  [on_device(): lax.psum((grad_msg_var_part, grad_con_part, grad_msg_con_part, grad_var_p...]
    dot_general x16 -> x0, matrix products: 53.3 us -> none  [the longest x1 8.02 us: on_device(): jnp.einsum('tij,tjd->tid', tile_values, tile_u, preferred_element_type=jn...]
    psum x1 -> x0, blocking collectives: 48.6 us -> none  [on_device(): lax.psum((grad_msg_var_part, grad_con_part, grad_msg_con_part, grad_var_p...]
    all_to_all x3 -> x1, starting transfers between devices: 44.2 us -> 7.39 us  [on_device(): lax.all_to_all(asked.reshape(n, cap), 'graph', split_axis=0, concat_axis=...]
    gather x6 -> x0, local copies, waits for them, and re-layouts: 22.3 us -> none  [the longest x2 6.79 us: to_slots(): picked = jnp.take(blocks, safe, axis=0)]
    dot_general x4 -> x0, local copies, waits for them, and re-layouts: 19.9 us -> none  [the longest x1 9.18 us: on_device(): jnp.einsum('tij,tjd->tid', tile_values, tile_u, preferred_element_type=jn...]
  transfers between devices with their start and end apart: 4 -> 1, of which waited for: 4 -> 1; matrix products, arithmetic and copies ran while one was open for 1% -> 1% of each run, Pallas kernels for 0% -> 0%
where the time goes in v1:
time: 357 us; the launch traced here: 355 us
  Pallas kernels  330 us (92%)
  starting transfers between devices  7.39 us (2%)
  local copies, waits for them, and re-layouts  7.28 us (2%)
  other arithmetic  6.86 us (2%)
    pallas_call x1, Pallas kernels, on_device(): pl.pallas_call(functools.partial(kernel, n, cap), out_shape=(jax.ShapeDty...  330 us
    all_to_all x1, starting transfers between devices, on_device(): lax.all_to_all(asked.reshape(n, cap), 'graph', split_axis=0, concat_axis=...  7.39 us
  transfers between devices with their start and end apart: 1, of which 1 were waited for; matrix products, arithmetic and copies ran while one was open for 1% of the time, Pallas kernels for 0%

profile of v1, /device:TPU:0, one launch (start us, length us, event | category | flops | bytes accessed | tf_op | source)
XLA Modules:
  0.0 354.8 jit_solution(3457586438279420024)
XLA Ops:
  0.6 0.9 convert_reduce_fusion
  1.5 0.7 fusion.1
  2.2 0.7 iota_add_fusion
  2.9 1.3 select_reduce_fusion
  4.2 0.7 sub.10
  4.8 7.4 %all-to-all-start = ((s32[16,1,4]{2,1,0:T(1,128)}), s32[16,1,4]{2,1,0:T(1,128)S(1)}, u32[]{:S(2)}, u32[]{:S(2)}) async-start(s32[16,1,4]{2,1,0:T(1,128)} %bitcast.3), calls=%async_computation | async-start | bytes 16384 | tf_op jit(solution)/shard_map/all_to_all | solution.py:394
  12.2 0.5 broadcast_add_fusion.1.slot_tile
  12.7 1.2 reshape.73
  14.0 2.1 copy.22.labels
  16.0 2.5 all-to-all-done
  18.6 0.5 broadcast.34
  19.1 0.7 reduce.4
  19.8 0.6 reshape.66.asked_of_me
  20.4 330.1 %shard_map.163 = (f32[16,128,1]{2,1,0:T(8,128)}, bf16[16,64,256]{2,1,0:T(8,128)(2,1)}, f32[8,256]{1,0:T(8,128)}) custom-call(s32[64]{0:T(128)} %broadcast_add_fusion.1.slot_tile, s32[64]{0:T(128)} %get-tuple-element.13.slot_row, s32[64]{0:T(128)} %reshape.66.asked_of_me, bf16[16,128,256]{2,1,0:T(8,128)(2,1)} %bitcast.18, bf16[8,128,256]{2,1,0:T(8,128)(2,1)} %bitcast.19, ...), custom_call_target="tpu_custom_call" | custom-call | tf_op jit(solution)/shard_map/pallas_call | solution.py:403
  350.4 0.0 copy-start
  350.4 1.3 slice.23
  351.8 2.1 fusion.2
  353.9 0.0 copy-done
  353.9 0.9 reduce.1
  (1 shorter events, 0.0 us)
Async XLA Ops:
  4.8 13.7 %all-to-all-start = ((s32[16,1,4]{2,1,0:T(1,128)}), s32[16,1,4]{2,1,0:T(1,128)S(1)}, u32[]{:S(2)}, u32[]{:S(2)}) async-start(s32[16,1,4]{2,1,0:T(1,128)} %bitcast.3), calls=%async_computation | async-start | bytes 16384 | tf_op jit(solution)/shard_map/all_to_all | solution.py:394
  350.4 3.4 copy-start

commit v2 on v1

--- a/solution.py
+++ b/solution.py
@@ -75,17 +75,18 @@
     blocks_c = con_feat.shape[0]
     scale = 1.0 / jnp.sqrt(jnp.float32(n * blocks_v * EDGE))
     turned = feat_t.shape[0] == n
+    stride = 5 if n % 5 else 1
 
     def each_peer(body):
         def step(i, carry):
-            body(lax.rem(me + i, n))
+            body(lax.rem(me + stride * i, n))
             return carry
 
         lax.fori_loop(1, n, step, 0)
 
     def each_sender(body):
         def step(i, carry):
-            body(lax.rem(me + n - i, n))
+            body(lax.rem(me + stride * (n - i), n))
             return carry
 
         lax.fori_loop(1, n, step, 0)

time: 357 us -> 343 us (0.961)
  Pallas kernels: 330 us -> 317 us
    pallas_call x1, Pallas kernels: 330 us -> 317 us  [on_device(): pl.pallas_call(functools.partial(kernel, n, cap), out_shape=(jax.ShapeDty...]
where the time goes in v2:
time: 343 us; the launch traced here: 342 us
  Pallas kernels  317 us (92%)
  starting transfers between devices  7.39 us (2%)
  local copies, waits for them, and re-layouts  7.28 us (2%)
  other arithmetic  6.86 us (2%)
    pallas_call x1, Pallas kernels, on_device(): pl.pallas_call(functools.partial(kernel, n, cap), out_shape=(jax.ShapeDty...  317 us
    all_to_all x1, starting transfers between devices, on_device(): lax.all_to_all(asked.reshape(n, cap), 'graph', split_axis=0, concat_axis=...  7.39 us
  transfers between devices with their start and end apart: 1, of which 1 were waited for; matrix products, arithmetic and copies ran while one was open for 1% of the time, Pallas kernels for 0%

profile of v2, /device:TPU:0, one launch (start us, length us, event | category | flops | bytes accessed | tf_op | source)
XLA Modules:
  0.0 342.2 jit_solution(11801345679303512256)
XLA Ops:
  0.6 0.9 convert_reduce_fusion
  1.5 0.7 fusion.1
  2.2 0.7 iota_add_fusion
  2.9 1.3 select_reduce_fusion
  4.2 0.7 sub.10
  4.8 7.4 %all-to-all-start = ((s32[16,1,4]{2,1,0:T(1,128)}), s32[16,1,4]{2,1,0:T(1,128)S(1)}, u32[]{:S(2)}, u32[]{:S(2)}) async-start(s32[16,1,4]{2,1,0:T(1,128)} %bitcast.3), calls=%async_computation | async-start | bytes 16384 | tf_op jit(solution)/shard_map/all_to_all | solution.py:395
  12.2 0.5 broadcast_add_fusion.1.slot_tile
  12.7 1.2 reshape.73
  14.0 2.1 copy.22.labels
  16.0 2.5 all-to-all-done
  18.6 0.5 broadcast.34
  19.1 0.7 reduce.4
  19.8 0.6 reshape.66.asked_of_me
  20.4 317.5 %shard_map.163 = (f32[16,128,1]{2,1,0:T(8,128)}, bf16[16,64,256]{2,1,0:T(8,128)(2,1)}, f32[8,256]{1,0:T(8,128)}) custom-call(s32[64]{0:T(128)} %broadcast_add_fusion.1.slot_tile, s32[64]{0:T(128)} %get-tuple-element.13.slot_row, s32[64]{0:T(128)} %reshape.66.asked_of_me, bf16[16,128,256]{2,1,0:T(8,128)(2,1)} %bitcast.18, bf16[8,128,256]{2,1,0:T(8,128)(2,1)} %bitcast.19, ...), custom_call_target="tpu_custom_call" | custom-call | tf_op jit(solution)/shard_map/pallas_call | solution.py:404
  337.9 0.0 copy-start
  337.9 1.3 slice.23
  339.2 2.1 fusion.2
  341.3 0.0 copy-done
  341.3 0.9 reduce.1
  (1 shorter events, 0.0 us)
Async XLA Ops:
  4.8 13.7 %all-to-all-start = ((s32[16,1,4]{2,1,0:T(1,128)}), s32[16,1,4]{2,1,0:T(1,128)S(1)}, u32[]{:S(2)}, u32[]{:S(2)}) async-start(s32[16,1,4]{2,1,0:T(1,128)} %bitcast.3), calls=%async_computation | async-start | bytes 16384 | tf_op jit(solution)/shard_map/all_to_all | solution.py:395
  337.9 3.4 %copy-start = (f32[16,128,1]{2,1,0:T(8,128)S(1)}, f32[16,128,1]{2,1,0:T(8,128)}, u32[]{:S(2)}) copy-start(f32[16,128,1]{2,1,0:T(8,128)} %get-tuple-element.9) | copy-start | bytes 24580
